TPU v7x, 512 devices: a whole 4x4x16 slice. The times are simulated.
512 devices in a mesh: ctx: 128 (over z, y_lo, x), head: 4 (over y_hi, core).
Axes of the slice: x: 4, y: 4 (y_hi: 2, y_lo: 2; y = y_hi * 2 + y_lo), z: 16, core: 2. Of those that a mesh axis runs over, the one named last changes fastest.
Arguments:
- cache_latent: bfloat16 [2, 32768, 576], P(None, 'ctx'), may hold values from -8 to 8
- group_latent: bfloat16 [2, 1024, 576], P(None, 'ctx'), may hold values from -8 to 8
- group_query: bfloat16 [2, 1024, 3072], P(None, 'ctx', 'head'), may hold values from -8 to 8
- decode_query: bfloat16 [2, 2, 8, 3072], P(None, None, None, 'head'), may hold values from -8 to 8
- group_start: int32 [2], replicated, may hold values from 16384 to 32768, as said below
- w_key: bfloat16 [512, 2048], P(None, 'head'), may hold values from -0.25 to 0.25
- w_value: bfloat16 [512, 2048], P(None, 'head'), may hold values from -0.25 to 0.25
- w_out: bfloat16 [2048, 2048], P('head'), may hold values from -0.125 to 0.125
Outputs:
- group_hidden: bfloat16 [2, 1024, 2048], P(None, 'ctx', 'head')
- decode_hidden: bfloat16 [2, 2, 8, 2048], P(None, None, None, 'head')
Inputs may be any that keep to these rules, and one draw needn't show every extreme that they name: Cache positions below group_start[b] hold request b's context; in every draw exactly one request has 32768, every other fewer.
All inputs are finite; a program needn't handle non-finite values.
Results may differ from a plain program's by a relative error of at most 0.015.
Values may be sent and summed in bfloat16 or wider, within the bound.
A program may use at most 64 MiB of HBM per device.

v0:
```python
import jax
import jax.numpy as jnp
from jax import lax
from jax.sharding import PartitionSpec as P

D_LAT = 512
D_ROPE = 64
D_NOPE = 128
D_V = 128


very_low = -1e30


def attend_block(carry, queries, key_rows, value_rows, rope_part, query_pos):
    row_peak, row_total, mixture = carry
    count = key_rows.shape[1]
    score_scale = 1.0 / (D_NOPE + D_ROPE) ** 0.5
    scores = jnp.einsum(
        "rqhd,rkhd->rqhk", queries[..., :D_NOPE], key_rows, preferred_element_type=jnp.float32
    )
    scores = scores + jnp.einsum(
        "rqhd,rkd->rqhk", queries[..., D_NOPE:], rope_part, preferred_element_type=jnp.float32
    )
    scores = scores * score_scale
    key_pos = jnp.arange(count, dtype=jnp.int32)
    allowed = (key_pos[None, :] <= query_pos[:, None])[None, :, None, :]
    scores = jnp.where(allowed, scores, very_low)
    new_peak = jnp.maximum(row_peak, jnp.max(scores, axis=-1))
    weights = jnp.where(allowed, jnp.exp(scores - new_peak[..., None]), 0.0)
    row_total = jnp.sum(weights, axis=-1)
    mixture = jnp.einsum(
        "rqhk,rkhd->rqhd",
        weights.astype(jnp.bfloat16),
        value_rows,
        preferred_element_type=jnp.float32,
    )
    return (new_peak, row_total, mixture)


def rescale_parts(own_peak, whole_peak, row_total, mixture):
    factor = jnp.exp(own_peak - whole_peak)
    return (row_total * factor, mixture * factor[..., None])


def shards(
    cache_latent, group_latent, group_query, decode_query, group_start, w_key, w_value, w_out
):
    requests = group_latent.shape[0]
    own_rows = group_latent.shape[1]
    context_rows = cache_latent.shape[1]
    local_heads = w_key.shape[1] // D_NOPE
    wide = D_NOPE + D_ROPE
    score_scale = 1.0 / wide**0.5
    queries = group_query.reshape(requests, own_rows, local_heads, wide)
    query_pos = lax.axis_index("ctx") * own_rows + jnp.arange(own_rows, dtype=jnp.int32)
    start_state = (
        jnp.full((requests, own_rows, local_heads), very_low, jnp.float32),
        jnp.zeros((requests, own_rows, local_heads), jnp.float32),
        jnp.zeros((requests, own_rows, local_heads, D_V), jnp.float32),
    )

    def expand_rows(latent_rows, weight, width):
        count = latent_rows.shape[1]
        flat_rows = latent_rows[..., :D_LAT].reshape(-1, D_LAT)
        product = jnp.dot(flat_rows, weight, preferred_element_type=jnp.float32).astype(
            jnp.bfloat16
        )
        return product.reshape(requests, count, local_heads, width)

    piece = lax.all_gather(group_latent, "ctx", axis=1, tiled=True)
    state = attend_block(
        start_state,
        queries,
        expand_rows(piece, w_key, D_NOPE),
        expand_rows(piece, w_value, D_V),
        piece[..., D_LAT:],
        query_pos,
    )
    group_attention = (state[2] / state[1][..., None]).astype(jnp.bfloat16)
    group_attention = group_attention.reshape(requests * own_rows, local_heads * D_V)
    cache_pos = lax.axis_index("ctx") * context_rows + jnp.arange(context_rows, dtype=jnp.int32)
    key_valid = jnp.concatenate(
        [cache_pos[None, :] < group_start[:, None], jnp.ones((requests, own_rows), jnp.bool_)],
        axis=1,
    )
    key_mask = key_valid[:, None, None, :]
    key_all = jnp.concatenate([cache_latent, group_latent], axis=1)
    key_latent = key_all[..., :D_LAT]
    key_rope = key_all[..., D_LAT:]
    absorb_key = w_key.reshape(D_LAT, local_heads, D_NOPE)
    value_wide = w_value.astype(jnp.float32).reshape(D_LAT, local_heads, D_V)
    step_count = decode_query.shape[0]
    finished = []
    for step_index in range(step_count):
        by_head = decode_query[step_index].reshape(requests, -1, local_heads, wide)
        absorbed = jnp.einsum(
            "rqhd,chd->rqhc", by_head[..., :D_NOPE], absorb_key, preferred_element_type=jnp.float32
        ).astype(jnp.bfloat16)
        scores = jnp.einsum(
            "rqhc,rkc->rqhk", absorbed, key_latent, preferred_element_type=jnp.float32
        )
        scores = scores + jnp.einsum(
            "rqhd,rkd->rqhk", by_head[..., D_NOPE:], key_rope, preferred_element_type=jnp.float32
        )
        scores = jnp.where(key_mask, scores * score_scale, very_low)
        row_peak = jnp.max(scores, axis=-1)
        weights = jnp.where(key_mask, jnp.exp(scores - row_peak[..., None]), 0.0)
        decode_row_total = jnp.sum(weights, axis=-1)
        decode_mixture = jnp.einsum(
            "rqhk,rkc->rqhc",
            weights.astype(jnp.bfloat16),
            key_latent,
            preferred_element_type=jnp.float32,
        )
        whole_peak = lax.pmax(row_peak, "ctx")
        scaled_total, scaled_mix = rescale_parts(
            row_peak, whole_peak, decode_row_total, decode_mixture
        )
        summed = lax.psum((scaled_total, scaled_mix), "ctx")
        mixture = summed[1]
        mixture = mixture / summed[0][..., None]
        attention = jnp.einsum(
            "...hc,chd->...hd", mixture, value_wide, precision=lax.Precision.HIGHEST
        )
        finished.append(attention.astype(jnp.bfloat16))
    decoded = jnp.stack(finished)
    decode_flat = decoded.reshape(-1, local_heads * D_V)
    group_terms = jnp.dot(group_attention, w_out, preferred_element_type=jnp.float32)
    decode_terms = jnp.dot(decode_flat, w_out, preferred_element_type=jnp.float32)
    group_share, decode_share = (
        lax.psum_scatter(
            group_terms.astype(jnp.bfloat16), "head", scatter_dimension=1, tiled=True
        ).astype(jnp.float32),
        lax.psum_scatter(
            decode_terms.astype(jnp.bfloat16), "head", scatter_dimension=1, tiled=True
        ).astype(jnp.float32),
    )
    out_width = group_share.shape[1]
    group_hidden = group_share.astype(jnp.bfloat16).reshape(requests, own_rows, out_width)
    decode_hidden = decode_share.astype(jnp.bfloat16).reshape(step_count, requests, -1, out_width)
    return (group_hidden, decode_hidden)


def solution(mesh):
    in_specs = (
        P(None, "ctx", None),
        P(None, "ctx", None),
        P(None, "ctx", "head"),
        P(None, None, None, "head"),
        P(),
        P(None, "head"),
        P(None, "head"),
        P("head", None),
    )
    out_specs = (P(None, "ctx", "head"), P(None, None, None, "head"))
    return jax.shard_map(shards, mesh=mesh, in_specs=in_specs, out_specs=out_specs, check_vma=False)
```

profile of v0, /device:TPU:1, one launch (start us, length us, event | category | flops | bytes accessed | tf_op | source)
XLA Modules:
  0.0 2082.1 jit_solution(17243809588880981235)
XLA Ops:
  7.2 0.0 copy-start
  7.2 0.0 all-reduce.6.cloned.1.call-start
  7.2 0.9 fusion.81
  8.1 0.1 reshape_squeeze.7
  8.3 0.1 reshape_squeeze.6
  8.4 0.6 slice.53
  9.0 1.4 copy.49
  10.4 0.7 fusion.49
  11.2 2.2 fusion.18
  13.4 1.6 fusion.16
  15.0 0.1 broadcast_compare_fusion
  15.1 1.1 fusion.84
  16.2 0.8 fusion.83
  17.1 265.1 %all-reduce.3 = (f32[2,8,4]{1,2,0:T(4,128)S(1)}, f32[2,8,4]{1,2,0:T(4,128)S(1)}) all-reduce(f32[2,8,4]{1,2,0:T(4,128)S(1)} %get-tuple-element.22, f32[2,8,4]{1,2,0:T(4,128)S(1)} %get-tuple-element.20), channel_id=1, replica_groups=mesh['ctx'=128,'head'=4] {'ctx'}, use_global_device_ids=true, to_apply=%region_9.10 | all-reduce | flops 128 | bytes 1024 | tf_op jit(solution)/shard_map/pmax | solution.py:116
  282.2 1.1 fusion.60
  283.3 0.9 convolution_multiply_fusion.1
  284.2 0.9 convolution_multiply_fusion
  285.1 0.0 all-reduce.6.cloned.1.call-update
  285.1 0.0 all-gather.2.cloned.1.call-start
  285.1 0.6 copy.40
  285.7 0.1 all-gather.2.cloned.1.call-update
  285.8 0.0 reduce-scatter.5.cloned.1.call-start
  285.9 0.8 reshape.76
  286.7 0.1 reshape.80
  286.9 256.3 %all-reduce.1 = (f32[2,8,4]{1,2,0:T(4,128)S(1)}, f32[2,8,4]{1,2,0:T(4,128)S(1)}) all-reduce(f32[2,8,4]{1,2,0:T(4,128)S(1)} %bitcast.132, f32[2,8,4]{1,2,0:T(4,128)S(1)} %bitcast.131), channel_id=1, replica_groups=mesh['ctx'=128,'head'=4] {'ctx'}, use_global_device_ids=true, to_apply=%region_12.13 | all-reduce | flops 128 | bytes 1024 | tf_op jit(solution)/shard_map/psum | solution.py:120
  543.3 0.1 iota_compare_fusion
  543.3 798.4 %all-reduce.6.cloned.1.call-done = (f32[2,8,4,512]{3,1,0,2:T(8,128)}, f32[2,8,4,512]{3,1,0,2:T(8,128)}) async-done(((f32[2,8,4,512]{3,1,0,2:T(8,128)}, f32[2,8,4,512]{3,1,0,2:T(8,128)}), (f32[2,8,4,512]{3,1,0,2:T(8,128)}, f32[2,8,4,512]{3,1,0,2:T(8,128)})) %all-reduce.6.cloned.1.call-update) | async-done | bytes 262160 | tf_op jit(solution)/shard_map/psum | solution.py:120
  1341.7 1.3 fusion.29
  1343.0 1.3 fusion.28
  1344.4 1.1 convolution_convert_fusion.2
  1345.5 0.0 reduce-scatter.5.cloned.1.call-update
  1345.5 0.0 reduce-scatter.3.cloned.1.call-start
  1345.6 554.9 %all-gather.2.cloned.1.call-done = bf16[2,1024,576]{2,0,1:T(2,128)(2,1)} async-done(((bf16[2,8,576]{2,0,1:T(2,128)(2,1)}), bf16[2,1024,576]{2,0,1:T(2,128)(2,1)}) %all-gather.2.cloned.1.call-update) | async-done | bytes 2359312 | tf_op jit(solution)/shard_map/all_gather | solution.py:71
  1900.5 1.6 slice-done
  1902.1 0.3 copy.79
  1902.4 0.7 copy-done.1
  1903.1 2.6 convolution_convert_fusion
  1905.7 2.6 convolution_convert_fusion.1
  1908.3 0.4 copy.82
  1908.7 4.0 reshape.74
  1912.7 4.0 reshape.75
  1916.7 2.2 fusion.6
  1918.9 0.3 fusion.82
  1919.2 0.2 fusion.47
  1919.4 3.0 convolution_convert_fusion.3
  1922.4 0.0 reduce-scatter.3.cloned.1.call-update
  1922.4 108.4 %reduce-scatter.5.cloned.1.call-done = bf16[32,512]{1,0:T(8,128)(2,1)} async-done(((bf16[32,2048]{1,0:T(8,128)(2,1)}), bf16[32,512]{1,0:T(8,128)(2,1)}) %reduce-scatter.5.cloned.1.call-update) | async-done | bytes 32784 | tf_op jit(solution)/shard_map/reduce_scatter | solution.py:135
  2030.9 44.7 %reduce-scatter.3.cloned.1.call-done = bf16[16,512]{1,0:T(8,128)(2,1)} async-done(((bf16[16,2048]{1,0:T(8,128)(2,1)}), bf16[16,512]{1,0:T(8,128)(2,1)}) %reduce-scatter.3.cloned.1.call-update) | async-done | bytes 16400 | tf_op jit(solution)/shard_map/reduce_scatter | solution.py:132
  (38 shorter events, 0.2 us)
Async XLA Ops:
  7.2 1337.2 %copy-start = (bf16[512,2048]{1,0:T(8,128)(2,1)S(1)}, bf16[512,2048]{1,0:T(8,128)(2,1)}, u32[]{:S(2)}) copy-start(bf16[512,2048]{1,0:T(8,128)(2,1)} %param.15) | copy-start | bytes 6291460
  7.2 3.9 copy-start.3
  7.2 1334.5 %all-reduce.6.cloned.1.call-start = ((), (), s32[]{:S(2)}) async-start(), calls=%async_computation.5 | async-start | bytes 524288 | tf_op jit(solution)/shard_map/psum | solution.py:120
  8.2 2.1 copy-start.4
  8.4 2.0 copy-start.5
  10.4 4.6 copy-start.7
  11.2 3.9 slice-start.2
  11.2 5.1 slice-start.3
  13.4 273.3 %copy-start.2 = (bf16[512,512]{1,0:T(8,128)(2,1)S(1)}, bf16[512,512]{1,0:T(8,128)(2,1)}, u32[]{:S(2)}) copy-start(bf16[512,512]{1,0:T(8,128)(2,1)} %param.14) | copy-start | bytes 1572868
  285.1 1615.4 %all-gather.2.cloned.1.call-start = ((), (), s32[]{:S(2)}) async-start(), calls=%async_computation.2 | async-start | bytes 2641920 | tf_op jit(solution)/shard_map/all_gather | solution.py:71
  285.8 1745.0 %reduce-scatter.5.cloned.1.call-start = ((), (), s32[]{:S(2)}) async-start(), calls=%async_computation.4 | async-start | bytes 163840 | tf_op jit(solution)/shard_map/reduce_scatter | solution.py:135
  286.7 1058.8 %copy-start.6 = (bf16[2,8,4,192]{3,2,1,0:T(4,128)(2,1)}, bf16[2,8,4,192]{3,2,1,0:T(4,128)(2,1)S(1)}, u32[]{:S(2)}) copy-start(bf16[2,8,4,192]{3,2,1,0:T(4,128)(2,1)S(1)} %reshape.76) | copy-start | bytes 73732
  1345.5 730.0 %reduce-scatter.3.cloned.1.call-start = ((), (), s32[]{:S(2)}) async-start(), calls=%async_computation.3 | async-start | bytes 81920 | tf_op jit(solution)/shard_map/reduce_scatter | solution.py:132
  1900.5 1.6 slice-start
  1902.1 1.0 copy-start.1
  1905.7 2.6 slice-start.1
  1912.7 4.0 slice-start.4
  1916.7 2.2 slice-start.5
Sparse Core Ops, SparseCore 0:
  285.2 1056.4 all-reduce.5
  1344.0 556.3 all-gather.1
  1904.3 126.5 reduce-scatter.4
  2034.3 41.2 reduce-scatter.2
where the time goes:
time: 2080 us
  waiting for transfers between devices  1510 us (73%)
  blocking collectives  521 us (25%)
  matrix products  21.9 us (1%)
    psum x1, waiting for transfers between devices, shards(): summed = lax.psum((scaled_total, scaled_mix), 'ctx')  798 us
    all_gather x1, waiting for transfers between devices, shards(): piece = lax.all_gather(group_latent, 'ctx', axis=1, tiled=True)  555 us
    pmax x1, blocking collectives, shards(): whole_peak = lax.pmax(row_peak, 'ctx')  265 us
    psum x1, blocking collectives, shards(): summed = lax.psum((scaled_total, scaled_mix), 'ctx')  256 us
    reduce_scatter x1, waiting for transfers between devices, shards(): lax.psum_scatter(decode_terms.astype(jnp.bfloat16), 'head', scatter_dimen...  108 us
    reduce_scatter x1, waiting for transfers between devices, shards(): lax.psum_scatter(group_terms.astype(jnp.bfloat16), 'head', scatter_dimens...  44.7 us
  transfers between devices with their start and end apart: 4, of which 4 were waited for; matrix products, arithmetic and copies ran while one was open for 1% of the time, Pallas kernels for 0%

commit v1 on v0

v1 whole, which is shorter than its diff:
```python
import jax
import jax.numpy as jnp
from jax import lax
from jax.experimental import pallas as pl
from jax.experimental.pallas import tpu as pltpu
from jax.sharding import PartitionSpec as P

MESH = pl.DeviceIdType.MESH
BF = jnp.bfloat16
F32 = jnp.float32
LAT = 512
ROPE = 64
NOPE = 128
WIDE = NOPE + ROPE
HALF = 384
LOCAL = 4
NZ = 16
NXY = 8
SCALE = 1.0 / WIDE**0.5
LOW = -1e30


def dot(a, b):
    return lax.dot_general(a, b, (((1,), (0,)), ((), ())), preferred_element_type=F32)


def dot_t(a, b):
    return lax.dot_general(a, b, (((1,), (1,)), ((), ())), preferred_element_type=F32)


def iota(shape, axis):
    return lax.broadcasted_iota(jnp.int32, shape, axis)


def split(value, pieces):
    out = []
    for _ in range(pieces):
        head = value.astype(BF).astype(F32)
        out.append(head)
        value = value - head
    return out


def by_lane(shape, columns):
    lane = iota(shape, 1)
    tile = jnp.zeros(shape, F32)
    for at, column in columns.items():
        tile = jnp.where(lane == at, column, tile)
    return tile


def merge(stats, at, blocks):
    peak = stats[..., at : at + 1] + stats[..., at + 1 : at + 2] + stats[..., at + 2 : at + 3]
    total = stats[..., at + 3 : at + 4] + stats[..., at + 4 : at + 5]
    top = jnp.max(peak, axis=0, keepdims=True)
    factor = jnp.exp(peak - top)
    return top[0], jnp.sum(factor * total, axis=0), jnp.sum(factor * blocks, axis=0)


def kernel(
    start_ref, cache_hbm, glat_hbm, gq_hbm, dq_hbm, wk_hbm, wv_hbm, wo_hbm,
    group_out, decode_out,
    cache, glat, gq, dq, wk, wv, wo,
    keys, queries, big_q, dsend, drecv, zrecv, psend, precv, gsend, grecv, hsend, hrecv,
    local_sem, send_sem, recv_sem,
):
    ctx = lax.axis_index("ctx")
    head = lax.axis_index("head")
    z = ctx // NXY
    xy = ctx % NXY
    yl = xy // 4
    x = xy % 4
    core = head % 2
    sibling = head // 2 * 2 + (1 - core)

    def xy_device(rel):
        dy, dx = rel // 4, rel % 4
        return z * NXY + (yl + dy) % 2 * 4 + (x + dx) % 4

    def back(rel):
        return rel // 4 * 4 + (4 - rel % 4) % 4

    def z_device(d):
        return (z + d + NZ) % NZ * NXY + xy

    def absolute(rel):
        return (yl + rel // 4) % 2 * 4 + (x + rel % 4) % 4

    def remote(src, dst, phase, device):
        pltpu.make_async_remote_copy(
            src_ref=src, dst_ref=dst, send_sem=send_sem.at[phase], recv_sem=recv_sem.at[phase],
            device_id=device, device_id_type=MESH,
        ).start()

    def took(ref, sem):
        pltpu.make_async_copy(ref, ref, sem).wait()

    loads = {}
    for at, (name, src, dst) in enumerate((
        ("glat", glat_hbm, glat), ("gq", gq_hbm, gq), ("dq", dq_hbm, dq), ("wk", wk_hbm, wk),
        ("cache", cache_hbm, cache), ("wv", wv_hbm, wv), ("wo", wo_hbm, wo),
    )):
        loads[name] = pltpu.make_async_copy(src, dst, local_sem.at[at])
        loads[name].start()
    barrier = pltpu.get_barrier_semaphore()

    def greet(device):
        pl.semaphore_signal(barrier, inc=1, device_id=device, device_id_type=MESH)

    for d in (4, 3, 2, 1):
        greet((z_device(d), head))
        greet((z_device(-d), head))
    for rel in range(1, NXY):
        greet((xy_device(rel), head))
    for rel in range(1, 4):
        greet((ctx, (head + rel) % 4))

    loads["glat"].wait()
    own = glat[...].astype(F32).reshape(16, LAT + ROPE).astype(BF)
    keys[0, 8] = own[:, :HALF]
    keys[1, 8] = jnp.concatenate(
        [own[:, HALF:], jnp.zeros((16, 2 * HALF - LAT - ROPE), BF)], axis=1
    )
    loads["gq"].wait()
    queries[0] = gq[...].astype(F32).reshape(16, LOCAL * WIDE).astype(BF)

    loads["dq"].wait()
    rows = NXY * 16
    flat = dq[...].astype(F32).reshape(32, LOCAL * WIDE).astype(BF)
    row = iota((rows, 32), 0)
    pick = absolute(row // 16) * 4 + row % 4 == iota((rows, 32), 1)
    spread = dot(jnp.where(pick, 1.0, 0.0).astype(BF), flat)
    row = iota((rows, 1), 0)
    row_head = row // 4 % 4
    row_req = absolute(row // 16) // 2 % 2
    nope = jnp.concatenate(
        [
            jnp.where(row_head == h, spread[:, h * WIDE : h * WIDE + NOPE], 0.0)
            for h in range(LOCAL)
        ],
        axis=1,
    ).astype(BF)
    rope = jnp.zeros((rows, ROPE), F32)
    for h in range(LOCAL):
        rope = jnp.where(row_head == h, spread[:, h * WIDE + NOPE : (h + 1) * WIDE], rope)
    rope = rope.astype(BF)
    loads["wk"].wait()
    absorbed = dot_t(nope, wk[...]).astype(BF)

    pl.semaphore_wait(barrier, 18)
    for d in (4, 3, 2, 1):
        remote(keys.at[core, 8], keys.at[core, 8 - d], 0, (z_device(d), head))
        remote(keys.at[core, 8], keys.at[core, 8 + d], 1, (z_device(-d), head))
    for rel in range(NXY - 1, 0, -1):
        remote(queries.at[0], queries.at[back(rel)], 2, (xy_device(rel), head))

    loads["cache"].wait()
    scores = []
    masks = []
    for r in range(2):
        got = dot_t(absorbed, cache[r, :, :LAT]) + dot_t(rope, cache[r, :, LAT:])
        position = ctx * 256 + iota((1, 256), 1)
        allowed = (position < start_ref[r]) & (row_req == r)
        masks.append(allowed)
        scores.append(jnp.where(allowed, got * SCALE, LOW))
    got = dot_t(absorbed, own[:, :LAT]) + dot_t(rope, own[:, LAT:])
    allowed = iota((1, 16), 1) // 8 == row_req
    masks.append(allowed)
    scores.append(jnp.where(allowed, got * SCALE, LOW))
    peak = jnp.max(scores[0], axis=1, keepdims=True)
    for got in scores[1:]:
        peak = jnp.maximum(peak, jnp.max(got, axis=1, keepdims=True))
    total = jnp.zeros((rows, 1), F32)
    mixture = jnp.zeros((rows, LAT), F32)
    for got, allowed, latent in zip(
        scores, masks, (cache[0, :, :LAT], cache[1, :, :LAT], own[:, :LAT])
    ):
        weights = jnp.where(allowed, jnp.exp(got - peak), 0.0)
        total = total + jnp.sum(weights, axis=1, keepdims=True)
        mixture = mixture + dot(weights.astype(BF), latent)
    loads["wv"].wait()
    wide = dot(mixture.astype(BF), wv[...])
    part = jnp.zeros((rows, NOPE), F32)
    for h in range(LOCAL):
        part = jnp.where(row_head == h, wide[:, h * 128 : (h + 1) * 128], part)
    stats = by_lane((rows, 128), dict(enumerate(split(peak, 3) + split(total, 2))))
    packed = jnp.concatenate([part, stats], axis=1).astype(BF).reshape(NXY, 16, 256)
    dsend[...] = packed
    drecv[0] = packed[0]
    for rel in range(NXY - 1, 0, -1):
        remote(dsend.at[rel], drecv.at[back(rel)], 3, (xy_device(rel), head))

    took(queries.at[1:NXY], recv_sem.at[2])
    all_q = queries[...].reshape(128, LOCAL * WIDE)
    for h in range(LOCAL):
        block = dot_t(all_q[:, h * WIDE : h * WIDE + NOPE], wk[:, h * 128 : (h + 1) * 128])
        big_q[h * 128 : (h + 1) * 128, :LAT] = block.astype(BF)
        big_q[h * 128 : (h + 1) * 128, LAT:] = jnp.concatenate(
            [
                all_q[:, h * WIDE + NOPE : (h + 1) * WIDE],
                jnp.zeros((128, 2 * HALF - LAT - ROPE), BF),
            ],
            axis=1,
        )

    took(keys.at[0, 4:8], recv_sem.at[0])
    took(keys.at[0, 9:13], recv_sem.at[1])
    remote(keys.at[core, 4:8], keys.at[core, 0:4], 4, (z_device(4), head))
    remote(keys.at[core, 9:12], keys.at[core, 13:16], 5, (z_device(-4), head))
    remote(keys.at[core, 4:8], keys.at[core, 4:8], 6, (ctx, sibling))
    remote(keys.at[core, 9:13], keys.at[core, 9:13], 7, (ctx, sibling))

    took(drecv.at[1:NXY], recv_sem.at[3])
    packed = drecv[...].astype(F32)
    peak, total, part = merge(packed[..., 128:], 0, packed[..., :128])
    stats = by_lane((16, 128), dict(enumerate(split(peak, 3) + split(total, 2))))
    zrecv[0] = jnp.concatenate([part, stats], axis=1).astype(BF)

    def send_z(j, carry):
        d = 8 + (j % 2 * 2 - 1) * ((j + 1) // 2)
        remote(zrecv.at[0], zrecv.at[NZ - d], 8, (z_device(d), head))
        return carry

    lax.fori_loop(0, NZ - 1, send_z, 0)

    took(keys.at[0, 0:4], recv_sem.at[4])
    took(keys.at[0, 13:16], recv_sem.at[5])
    remote(keys.at[core, 0:4], keys.at[core, 0:4], 9, (ctx, sibling))
    remote(keys.at[core, 13:16], keys.at[core, 13:16], 10, (ctx, sibling))
    took(keys.at[0, 4:8], recv_sem.at[6])
    took(keys.at[0, 9:13], recv_sem.at[7])
    took(keys.at[0, 0:4], recv_sem.at[9])
    took(keys.at[0, 13:16], recv_sem.at[10])

    first = keys[0].reshape(256, HALF)
    second = keys[1].reshape(256, HALF)
    scores = dot_t(big_q[:, :HALF], first) + dot_t(big_q[:, HALF:], second)
    row = iota((LOCAL * 128, 1), 0)
    col = iota((1, 256), 1)
    query_at = (z * NXY + absolute(row // 16 % NXY)) * 8 + row % 8
    key_at = ((z + col // 16 + 8) % NZ * NXY + xy) * 8 + col % 8
    allowed = (key_at <= query_at) & (row // 8 % 2 == col // 8 % 2)
    scores = jnp.where(allowed, scores * SCALE, LOW)
    peak = jnp.max(scores, axis=1, keepdims=True)
    weights = jnp.where(allowed, jnp.exp(scores - peak), 0.0)
    total = jnp.sum(weights, axis=1, keepdims=True)
    weights = weights.astype(BF)
    mixture = jnp.concatenate(
        [dot(weights, first), dot(weights, second[:, : LAT - HALF])], axis=1
    ).astype(BF)
    columns = {}
    for h in range(LOCAL):
        at = slice(h * 128, (h + 1) * 128)
        part = dot(mixture[at], wv[:, at]).astype(BF).reshape(NXY, 16, 128)
        gsend[:, :, at] = part
        grecv[0, :, at] = part[0]
        for k, column in enumerate(split(peak[at], 3) + split(total[at], 2)):
            columns[8 * h + k] = column
    stats = by_lane((128, 128), columns).astype(BF).reshape(NXY, 16, 128)
    gsend[:, :, LAT:] = stats
    grecv[0, :, LAT:] = stats[0]
    for rel in range(NXY - 1, 0, -1):
        remote(gsend.at[rel], grecv.at[back(rel)], 11, (xy_device(rel), head))

    took(zrecv.at[1:NZ], recv_sem.at[8])
    packed = zrecv[...].astype(F32)
    peak, total, part = merge(packed[..., 128:], 0, packed[..., :128])
    attention = (part / total).astype(BF)
    row = iota((64, 16), 0)
    pick = row // 16 * 4 + row % 4 == iota((64, 16), 1)
    spread = dot(jnp.where(pick, 1.0, 0.0).astype(BF), attention).astype(BF)
    lined = jnp.concatenate([spread[h * 16 : (h + 1) * 16] for h in range(LOCAL)], axis=1)
    loads["wo"].wait()
    hidden = dot(lined, wo[...])
    block = iota((16, 128), 0) // 4
    for j in range(4):
        tile = jnp.zeros((16, 128), F32)
        for c in range(4):
            at = j * 512 + c * 128
            tile = jnp.where(block == c, hidden[:, at : at + 128], tile)
        psend[j] = tile.astype(BF)
    precv[0] = psend[head]

    def send_plane(j, carry):
        k = 31 - j
        rel, turn = k // 4, k % 4
        there = (head + turn) % 4
        slot = back(rel) * 4 + (4 - turn) % 4
        remote(psend.at[there], precv.at[slot], 12, (xy_device(rel), there))
        return carry

    lax.fori_loop(0, 31, send_plane, 0)

    took(grecv.at[1:NXY], recv_sem.at[11])
    stats = grecv[:, :, LAT:].astype(F32)
    blocks = []
    for h in range(LOCAL):
        got = grecv[:, :, h * 128 : (h + 1) * 128].astype(F32)
        peak, total, part = merge(stats, 8 * h, got)
        blocks.append((part / total).astype(BF))
    hidden = dot(jnp.concatenate(blocks, axis=1), wo[...]).astype(BF)
    for j in range(4):
        hsend[j] = hidden[:, j * 512 : (j + 1) * 512]
    hrecv[0] = hsend[head]
    for turn in (2, 3, 1):
        there = (head + turn) % 4
        remote(hsend.at[there], hrecv.at[4 - turn], 13, (ctx, there))

    took(precv.at[1:32], recv_sem.at[12])
    summed = jnp.sum(precv[...].astype(F32).reshape(NXY, 4, 16, 128), axis=1)
    summed = summed.reshape(128, 128).astype(BF)
    row = iota((128, 128), 0)
    col = iota((128, 128), 1)
    pick = (row // 32 == col // 4 % 4) & (row % 32 == absolute(col // 16) * 4 + col % 4)
    placed = dot(jnp.where(pick, 1.0, 0.0).astype(BF), summed)
    decode_out[...] = (
        jnp.concatenate([placed[c * 32 : (c + 1) * 32] for c in range(4)], axis=1)
        .reshape(2, 2, 8, 512)
        .astype(BF)
    )
    took(hrecv.at[1:4], recv_sem.at[13])
    group_out[...] = (
        jnp.sum(hrecv[...].astype(F32), axis=0).reshape(2, 8, 512).astype(BF)
    )

    for phase, ref in (
        (0, keys.at[0, 4:8]), (1, keys.at[0, 9:13]), (2, queries.at[1:NXY]), (3, drecv.at[1:NXY]),
        (4, keys.at[0, 0:4]), (5, keys.at[0, 13:16]), (6, keys.at[0, 4:8]), (7, keys.at[0, 9:13]),
        (8, zrecv.at[1:NZ]), (9, keys.at[0, 0:4]), (10, keys.at[0, 13:16]),
        (11, grecv.at[1:NXY]), (12, precv.at[1:32]), (13, hrecv.at[1:4]),
    ):
        took(ref, send_sem.at[phase])


def shards(
    cache_latent, group_latent, group_query, decode_query, group_start, w_key, w_value, w_out
):
    anywhere = pl.BlockSpec(memory_space=pl.ANY)
    vmem = pl.BlockSpec(memory_space=pltpu.VMEM)
    return pl.pallas_call(
        kernel,
        out_shape=(
            jax.ShapeDtypeStruct((2, 8, 512), BF),
            jax.ShapeDtypeStruct((2, 2, 8, 512), BF),
        ),
        in_specs=[pl.BlockSpec(memory_space=pltpu.SMEM)] + [anywhere] * 7,
        out_specs=(vmem, vmem),
        scratch_shapes=[
            pltpu.VMEM((2, 256, 576), BF),
            pltpu.VMEM((2, 8, 576), BF),
            pltpu.VMEM((2, 8, 768), BF),
            pltpu.VMEM((2, 2, 8, 768), BF),
            pltpu.VMEM((512, 512), BF),
            pltpu.VMEM((512, 512), BF),
            pltpu.VMEM((512, 2048), BF),
            pltpu.VMEM((2, NZ, 16, HALF), BF),
            pltpu.VMEM((NXY, 16, 768), BF),
            pltpu.VMEM((512, 2 * HALF), BF),
            pltpu.VMEM((NXY, 16, 256), BF),
            pltpu.VMEM((NXY, 16, 256), BF),
            pltpu.VMEM((NZ, 16, 256), BF),
            pltpu.VMEM((4, 16, 128), BF),
            pltpu.VMEM((32, 16, 128), BF),
            pltpu.VMEM((NXY, 16, 640), BF),
            pltpu.VMEM((NXY, 16, 640), BF),
            pltpu.VMEM((4, 16, 512), BF),
            pltpu.VMEM((4, 16, 512), BF),
            pltpu.SemaphoreType.DMA((7,)),
            pltpu.SemaphoreType.DMA((14,)),
            pltpu.SemaphoreType.DMA((14,)),
        ],
        compiler_params=pltpu.CompilerParams(
            collective_id=0, has_side_effects=True, vmem_limit_bytes=32 << 20
        ),
        name="latent_attention",
    )(
        group_start, cache_latent, group_latent, group_query, decode_query, w_key, w_value, w_out
    )


def solution(mesh):
    in_specs = (
        P(None, "ctx", None),
        P(None, "ctx", None),
        P(None, "ctx", "head"),
        P(None, None, None, "head"),
        P(),
        P(None, "head"),
        P(None, "head"),
        P("head", None),
    )
    out_specs = (P(None, "ctx", "head"), P(None, None, None, "head"))
    return jax.shard_map(shards, mesh=mesh, in_specs=in_specs, out_specs=out_specs, check_vma=False)
```

time: 2080 us -> 50.7 us (0.02)
  waiting for transfers between devices: 1510 us -> 0 us
  blocking collectives: 521 us -> 0 us
  Pallas kernels: 0 us -> 40.4 us
  matrix products: 21.9 us -> 0 us
    psum x1 -> x0, waiting for transfers between devices: 798 us -> none  [shards(): summed = lax.psum((scaled_total, scaled_mix), 'ctx')]
    all_gather x1 -> x0, waiting for transfers between devices: 555 us -> none  [shards(): piece = lax.all_gather(group_latent, 'ctx', axis=1, tiled=True)]
    pmax x1 -> x0, blocking collectives: 265 us -> none  [shards(): whole_peak = lax.pmax(row_peak, 'ctx')]
    psum x1 -> x0, blocking collectives: 256 us -> none  [shards(): summed = lax.psum((scaled_total, scaled_mix), 'ctx')]
    reduce_scatter x2 -> x0, waiting for transfers between devices: 153 us -> none  [the longest x1 108 us: shards(): lax.psum_scatter(decode_terms.astype(jnp.bfloat16), 'head', scatter_dimen...]
    pallas_call x0 -> x1, Pallas kernels: none -> 40.4 us  [shards(): pl.pallas_call(kernel, out_shape=(jax.ShapeDtypeStruct((2, 8, 512), BF),...]
    dot_general x14 -> x0, matrix products: 21.9 us -> none  [the longest x2 5.21 us: expand_rows(): jnp.dot(flat_rows, weight, preferred_element_type=jnp.float32)]
  transfers between devices with their start and end apart: 4 -> 0, of which waited for: 4 -> 0; matrix products, arithmetic and copies ran while one was open for 1% -> 0% of each run, Pallas kernels for 0% -> 0%
where the time goes in v1:
time: 50.7 us; the launch traced here: 50.3 us
  Pallas kernels  40.4 us (80%)
  local copies, waits for them, and re-layouts  9.16 us (18%)
  between operations  0.66 us (1%)
    pallas_call x1, Pallas kernels, shards(): pl.pallas_call(kernel, out_shape=(jax.ShapeDtypeStruct((2, 8, 512), BF),...  40.4 us
    unnamed x17, local copies, waits for them, and re-layouts  9.16 us

profile of v1, /device:TPU:1, one launch (start us, length us, event | category | flops | bytes accessed | tf_op | source)
XLA Modules:
  0.0 50.3 jit_solution(17925803631658512496)
XLA Ops:
  0.6 1.4 %copy.10.cache_hbm = bf16[2,256,576]{2,1,0:T(8,128)(2,1)S(1)} copy(bf16[2,256,576]{1,2,0:T(8,128)(2,1)} %param.8) | data formatting | bytes 1179648 | tf_op args[0]
  2.0 0.0 copy-start
  2.0 1.6 %copy-done = bf16[512,2048]{1,0:T(8,128)(2,1)S(1)} copy-done((bf16[512,2048]{1,0:T(8,128)(2,1)S(1)}, bf16[512,2048]{1,0:T(8,128)(2,1)}, u32[]{:S(2)}) %copy-start) | copy-done | bytes 2097176
  3.6 0.0 copy-start.1
  3.6 1.0 %copy-done.1 = bf16[512,512]{1,0:T(8,128)(2,1)S(1)} copy-done((bf16[512,512]{1,0:T(8,128)(2,1)S(1)}, bf16[512,512]{1,0:T(8,128)(2,1)}, u32[]{:S(2)}) %copy-start.1) | copy-done | bytes 524312
  4.6 0.0 copy-start.2
  4.6 1.0 %copy-done.2 = bf16[512,512]{1,0:T(8,128)(2,1)S(1)} copy-done((bf16[512,512]{1,0:T(8,128)(2,1)S(1)}, bf16[512,512]{1,0:T(8,128)(2,1)}, u32[]{:S(2)}) %copy-start.2) | copy-done | bytes 524312
  5.7 0.0 copy-start.3
  5.7 0.8 %copy-done.3 = bf16[2,2,8,768]{3,2,1,0:T(8,128)(2,1)S(1)} copy-done((bf16[2,2,8,768]{3,2,1,0:T(8,128)(2,1)S(1)}, bf16[2,2,8,768]{3,2,1,0:T(8,128)(2,1)}, u32[]{:S(2)}) %copy-start.3) | copy-done | bytes 49176
  6.5 0.0 copy-start.4
  6.5 0.7 %copy-done.4 = bf16[2,8,768]{2,1,0:T(8,128)(2,1)S(1)} copy-done((bf16[2,8,768]{2,1,0:T(8,128)(2,1)S(1)}, bf16[2,8,768]{2,1,0:T(8,128)(2,1)}, u32[]{:S(2)}) %copy-start.4) | copy-done | bytes 24600
  7.2 0.0 copy-start.5
  7.2 0.7 %copy-done.5 = bf16[2,8,576]{2,1,0:T(8,128)(2,1)S(1)} copy-done((bf16[2,8,576]{2,1,0:T(8,128)(2,1)S(1)}, bf16[2,8,576]{2,1,0:T(8,128)(2,1)}, u32[]{:S(2)}) %copy-start.5) | copy-done | bytes 18456
  7.9 0.0 copy-start.6
  7.9 0.7 %copy-done.6 = s32[2]{0:T(128)S(1)} copy-done((s32[2]{0:T(128)S(1)}, s32[2]{0:T(128)}, u32[]{:S(2)}) %copy-start.6) | copy-done | bytes 32
  8.6 40.4 %latent_attention.1 = (bf16[2,8,512]{2,1,0:T(8,128)(2,1)S(1)}, bf16[2,2,8,512]{3,2,1,0:T(8,128)(2,1)S(1)}) custom-call(s32[2]{0:T(128)S(1)} %copy-done.6, bf16[2,256,576]{2,1,0:T(8,128)(2,1)S(1)} %copy.10.cache_hbm, bf16[2,8,576]{2,1,0:T(8,128)(2,1)S(1)} %copy-done.5, bf16[2,8,768]{2,1,0:T(8,128)(2,1)S(1)} %copy-done.4, ...), custom_call_target="tpu_custom_call" | custom-call | tf_op jit(solution)/shard_map/latent_attention/pallas_call | solution.py:340
  49.0 0.6 %copy.13 = bf16[2,8,512]{2,1,0:T(8,128)(2,1)} copy(bf16[2,8,512]{2,1,0:T(8,128)(2,1)S(1)} %get-tuple-element.4) | data formatting | bytes 32768
  49.6 0.6 %copy.14 = bf16[2,2,8,512]{3,2,1,0:T(8,128)(2,1)} copy(bf16[2,2,8,512]{3,2,1,0:T(8,128)(2,1)S(1)} %get-tuple-element.5) | data formatting | bytes 65536
Async XLA Ops:
  2.0 1.6 %copy-start = (bf16[512,2048]{1,0:T(8,128)(2,1)S(1)}, bf16[512,2048]{1,0:T(8,128)(2,1)}, u32[]{:S(2)}) copy-start(bf16[512,2048]{1,0:T(8,128)(2,1)} %wo_hbm.1) | copy-start | bytes 6291460
  3.6 1.0 %copy-start.1 = (bf16[512,512]{1,0:T(8,128)(2,1)S(1)}, bf16[512,512]{1,0:T(8,128)(2,1)}, u32[]{:S(2)}) copy-start(bf16[512,512]{1,0:T(8,128)(2,1)} %wk_hbm.1) | copy-start | bytes 1572868
  4.6 1.0 %copy-start.2 = (bf16[512,512]{1,0:T(8,128)(2,1)S(1)}, bf16[512,512]{1,0:T(8,128)(2,1)}, u32[]{:S(2)}) copy-start(bf16[512,512]{1,0:T(8,128)(2,1)} %wv_hbm.1) | copy-start | bytes 1572868
  5.7 0.8 %copy-start.3 = (bf16[2,2,8,768]{3,2,1,0:T(8,128)(2,1)S(1)}, bf16[2,2,8,768]{3,2,1,0:T(8,128)(2,1)}, u32[]{:S(2)}) copy-start(bf16[2,2,8,768]{3,2,1,0:T(8,128)(2,1)} %dq_hbm.1) | copy-start | bytes 147460
  6.5 0.7 %copy-start.4 = (bf16[2,8,768]{2,1,0:T(8,128)(2,1)S(1)}, bf16[2,8,768]{2,1,0:T(8,128)(2,1)}, u32[]{:S(2)}) copy-start(bf16[2,8,768]{2,1,0:T(8,128)(2,1)} %gq_hbm.1) | copy-start | bytes 73732
  7.2 0.7 %copy-start.5 = (bf16[2,8,576]{2,1,0:T(8,128)(2,1)S(1)}, bf16[2,8,576]{2,1,0:T(8,128)(2,1)}, u32[]{:S(2)}) copy-start(bf16[2,8,576]{2,1,0:T(8,128)(2,1)} %glat_hbm.1) | copy-start | bytes 55300
  7.9 0.7 %copy-start.6 = (s32[2]{0:T(128)S(1)}, s32[2]{0:T(128)}, u32[]{:S(2)}) copy-start(s32[2]{0:T(128)} %start_ref.1) | copy-start | bytes 28

commit v2 on v1

--- a/solution.py
+++ b/solution.py
@@ -58,11 +58,11 @@
 
 
 def kernel(
-    start_ref, cache_hbm, glat_hbm, gq_hbm, dq_hbm, wk_hbm, wv_hbm, wo_hbm,
+    start_hbm, cache_hbm, glat_hbm, gq_hbm, dq_hbm, wk_hbm, wv_hbm, wo_hbm,
     group_out, decode_out,
-    cache, glat, gq, dq, wk, wv, wo,
+    start, cache, glat, gq, dq, wk, wv, wo,
     keys, queries, big_q, dsend, drecv, zrecv, psend, precv, gsend, grecv, hsend, hrecv,
-    local_sem, send_sem, recv_sem,
+    local_sem, send_sem, recv_sem, key_send, key_recv, here,
 ):
     ctx = lax.axis_index("ctx")
     head = lax.axis_index("head")
@@ -81,7 +81,7 @@
         return rel // 4 * 4 + (4 - rel % 4) % 4
 
     def z_device(d):
-        return (z + d + NZ) % NZ * NXY + xy
+        return (z + d) % NZ * NXY + xy
 
     def absolute(rel):
         return (yl + rel // 4) % 2 * 4 + (x + rel % 4) % 4
@@ -98,18 +98,28 @@
     loads = {}
     for at, (name, src, dst) in enumerate((
         ("glat", glat_hbm, glat), ("gq", gq_hbm, gq), ("dq", dq_hbm, dq), ("wk", wk_hbm, wk),
-        ("cache", cache_hbm, cache), ("wv", wv_hbm, wv), ("wo", wo_hbm, wo),
+        ("start", start_hbm, start), ("cache", cache_hbm, cache), ("wv", wv_hbm, wv),
+        ("wo", wo_hbm, wo),
     )):
         loads[name] = pltpu.make_async_copy(src, dst, local_sem.at[at])
         loads[name].start()
+    keys[...] = jnp.zeros_like(keys)
     barrier = pltpu.get_barrier_semaphore()
 
     def greet(device):
         pl.semaphore_signal(barrier, inc=1, device_id=device, device_id_type=MESH)
 
-    for d in (4, 3, 2, 1):
-        greet((z_device(d), head))
-        greet((z_device(-d), head))
+    def ranked(r):
+        return r % 2 * ((r + 1) // 2) + (1 - r % 2) * ((NZ - r // 2) % NZ)
+
+    upper = z // 9
+    rank = 2 * (z + upper * (NZ - 2 * z)) - 1 + upper + (NZ - z) // NZ
+
+    def greet_z(r, carry):
+        greet((ranked(r) * NXY + xy, head))
+        return carry
+
+    lax.fori_loop(rank + 1, NZ, greet_z, 0)
     for rel in range(1, NXY):
         greet((xy_device(rel), head))
     for rel in range(1, 4):
@@ -117,12 +127,62 @@
 
     loads["glat"].wait()
     own = glat[...].astype(F32).reshape(16, LAT + ROPE).astype(BF)
-    keys[0, 8] = own[:, :HALF]
-    keys[1, 8] = jnp.concatenate(
+    keys[0, 0] = own[:, :HALF]
+    keys[1, 0] = jnp.concatenate(
         [own[:, HALF:], jnp.zeros((16, 2 * HALF - LAT - ROPE), BF)], axis=1
     )
+
+    def send_keys(there):
+        pltpu.make_async_remote_copy(
+            src_ref=keys.at[core, 0], dst_ref=keys.at[core, there - z],
+            send_sem=key_send.at[there - z], recv_sem=key_recv.at[there - z],
+            device_id=(there * NXY + xy, head), device_id_type=MESH,
+        ).start()
+
+    def to_lower(r, carry):
+        there = ranked(r)
+
+        @pl.when(there > z)
+        def _():
+            send_keys(there)
+
+        @pl.when(there < z)
+        def _():
+            pl.semaphore_signal(
+                here.at[z], inc=1, device_id=(there * NXY + xy, head), device_id_type=MESH
+            )
+
+        return carry
+
+    def to_higher(r, carry):
+        there = ranked(r)
+
+        @pl.when(there > z)
+        def _():
+            pl.semaphore_wait(here.at[there], 1)
+            send_keys(there)
+
+        @pl.when(there < z)
+        def _():
+            took(keys.at[0, 1], key_recv.at[z - there])
+
+        return carry
+
+    def from_lower(r, carry):
+        there = ranked(r)
+
+        @pl.when(there < z)
+        def _():
+            took(keys.at[0, 1], key_recv.at[z - there])
+
+        return carry
+
+    pl.semaphore_wait(barrier, 10 + rank)
+    lax.fori_loop(0, rank, to_lower, 0)
     loads["gq"].wait()
     queries[0] = gq[...].astype(F32).reshape(16, LOCAL * WIDE).astype(BF)
+    for rel in range(NXY - 1, 0, -1):
+        remote(queries.at[0], queries.at[back(rel)], 2, (xy_device(rel), head))
 
     loads["dq"].wait()
     rows = NXY * 16
@@ -147,20 +207,14 @@
     loads["wk"].wait()
     absorbed = dot_t(nope, wk[...]).astype(BF)
 
-    pl.semaphore_wait(barrier, 18)
-    for d in (4, 3, 2, 1):
-        remote(keys.at[core, 8], keys.at[core, 8 - d], 0, (z_device(d), head))
-        remote(keys.at[core, 8], keys.at[core, 8 + d], 1, (z_device(-d), head))
-    for rel in range(NXY - 1, 0, -1):
-        remote(queries.at[0], queries.at[back(rel)], 2, (xy_device(rel), head))
-
+    loads["start"].wait()
     loads["cache"].wait()
     scores = []
     masks = []
     for r in range(2):
-        got = dot_t(absorbed, cache[r, :, :LAT]) + dot_t(rope, cache[r, :, LAT:])
+        got = dot(absorbed, cache[r, :LAT]) + dot(rope, cache[r, LAT:])
         position = ctx * 256 + iota((1, 256), 1)
-        allowed = (position < start_ref[r]) & (row_req == r)
+        allowed = (position < start[r]) & (row_req == r)
         masks.append(allowed)
         scores.append(jnp.where(allowed, got * SCALE, LOW))
     got = dot_t(absorbed, own[:, :LAT]) + dot_t(rope, own[:, LAT:])
@@ -172,12 +226,13 @@
         peak = jnp.maximum(peak, jnp.max(got, axis=1, keepdims=True))
     total = jnp.zeros((rows, 1), F32)
     mixture = jnp.zeros((rows, LAT), F32)
-    for got, allowed, latent in zip(
-        scores, masks, (cache[0, :, :LAT], cache[1, :, :LAT], own[:, :LAT])
-    ):
+    for k, (got, allowed) in enumerate(zip(scores, masks)):
         weights = jnp.where(allowed, jnp.exp(got - peak), 0.0)
         total = total + jnp.sum(weights, axis=1, keepdims=True)
-        mixture = mixture + dot(weights.astype(BF), latent)
+        weights = weights.astype(BF)
+        mixture = mixture + (
+            dot_t(weights, cache[k, :LAT]) if k < 2 else dot(weights, own[:, :LAT])
+        )
     loads["wv"].wait()
     wide = dot(mixture.astype(BF), wv[...])
     part = jnp.zeros((rows, NOPE), F32)
@@ -203,12 +258,7 @@
             axis=1,
         )
 
-    took(keys.at[0, 4:8], recv_sem.at[0])
-    took(keys.at[0, 9:13], recv_sem.at[1])
-    remote(keys.at[core, 4:8], keys.at[core, 0:4], 4, (z_device(4), head))
-    remote(keys.at[core, 9:12], keys.at[core, 13:16], 5, (z_device(-4), head))
-    remote(keys.at[core, 4:8], keys.at[core, 4:8], 6, (ctx, sibling))
-    remote(keys.at[core, 9:13], keys.at[core, 9:13], 7, (ctx, sibling))
+    lax.fori_loop(rank + 1, NZ, to_higher, 0)
 
     took(drecv.at[1:NXY], recv_sem.at[3])
     packed = drecv[...].astype(F32)
@@ -218,19 +268,14 @@
 
     def send_z(j, carry):
         d = 8 + (j % 2 * 2 - 1) * ((j + 1) // 2)
-        remote(zrecv.at[0], zrecv.at[NZ - d], 8, (z_device(d), head))
+        remote(zrecv.at[0], zrecv.at[NZ - d], 1, (z_device(d), head))
         return carry
 
     lax.fori_loop(0, NZ - 1, send_z, 0)
 
-    took(keys.at[0, 0:4], recv_sem.at[4])
-    took(keys.at[0, 13:16], recv_sem.at[5])
-    remote(keys.at[core, 0:4], keys.at[core, 0:4], 9, (ctx, sibling))
-    remote(keys.at[core, 13:16], keys.at[core, 13:16], 10, (ctx, sibling))
-    took(keys.at[0, 4:8], recv_sem.at[6])
-    took(keys.at[0, 9:13], recv_sem.at[7])
-    took(keys.at[0, 0:4], recv_sem.at[9])
-    took(keys.at[0, 13:16], recv_sem.at[10])
+    lax.fori_loop(0, rank, from_lower, 0)
+    remote(keys.at[core, 1:NZ], keys.at[core, 1:NZ], 0, (ctx, sibling))
+    took(keys.at[0, 1:NZ], recv_sem.at[0])
 
     first = keys[0].reshape(256, HALF)
     second = keys[1].reshape(256, HALF)
@@ -238,8 +283,9 @@
     row = iota((LOCAL * 128, 1), 0)
     col = iota((1, 256), 1)
     query_at = (z * NXY + absolute(row // 16 % NXY)) * 8 + row % 8
-    key_at = ((z + col // 16 + 8) % NZ * NXY + xy) * 8 + col % 8
-    allowed = (key_at <= query_at) & (row // 8 % 2 == col // 8 % 2)
+    key_z = z - col // 16
+    key_at = (key_z * NXY + xy) * 8 + col % 8
+    allowed = (key_z >= 0) & (key_at <= query_at) & (row // 8 % 2 == col // 8 % 2)
     scores = jnp.where(allowed, scores * SCALE, LOW)
     peak = jnp.max(scores, axis=1, keepdims=True)
     weights = jnp.where(allowed, jnp.exp(scores - peak), 0.0)
@@ -260,9 +306,9 @@
     gsend[:, :, LAT:] = stats
     grecv[0, :, LAT:] = stats[0]
     for rel in range(NXY - 1, 0, -1):
-        remote(gsend.at[rel], grecv.at[back(rel)], 11, (xy_device(rel), head))
-
-    took(zrecv.at[1:NZ], recv_sem.at[8])
+        remote(gsend.at[rel], grecv.at[back(rel)], 4, (xy_device(rel), head))
+
+    took(zrecv.at[1:NZ], recv_sem.at[1])
     packed = zrecv[...].astype(F32)
     peak, total, part = merge(packed[..., 128:], 0, packed[..., :128])
     attention = (part / total).astype(BF)
@@ -286,12 +332,12 @@
         rel, turn = k // 4, k % 4
         there = (head + turn) % 4
         slot = back(rel) * 4 + (4 - turn) % 4
-        remote(psend.at[there], precv.at[slot], 12, (xy_device(rel), there))
+        remote(psend.at[there], precv.at[slot], 5, (xy_device(rel), there))
         return carry
 
     lax.fori_loop(0, 31, send_plane, 0)
 
-    took(grecv.at[1:NXY], recv_sem.at[11])
+    took(grecv.at[1:NXY], recv_sem.at[4])
     stats = grecv[:, :, LAT:].astype(F32)
     blocks = []
     for h in range(LOCAL):
@@ -304,9 +350,9 @@
     hrecv[0] = hsend[head]
     for turn in (2, 3, 1):
         there = (head + turn) % 4
-        remote(hsend.at[there], hrecv.at[4 - turn], 13, (ctx, there))
-
-    took(precv.at[1:32], recv_sem.at[12])
+        remote(hsend.at[there], hrecv.at[4 - turn], 6, (ctx, there))
+
+    took(precv.at[1:32], recv_sem.at[5])
     summed = jnp.sum(precv[...].astype(F32).reshape(NXY, 4, 16, 128), axis=1)
     summed = summed.reshape(128, 128).astype(BF)
     row = iota((128, 128), 0)
@@ -318,24 +364,28 @@
         .reshape(2, 2, 8, 512)
         .astype(BF)
     )
-    took(hrecv.at[1:4], recv_sem.at[13])
+    took(hrecv.at[1:4], recv_sem.at[6])
     group_out[...] = (
         jnp.sum(hrecv[...].astype(F32), axis=0).reshape(2, 8, 512).astype(BF)
     )
 
     for phase, ref in (
-        (0, keys.at[0, 4:8]), (1, keys.at[0, 9:13]), (2, queries.at[1:NXY]), (3, drecv.at[1:NXY]),
-        (4, keys.at[0, 0:4]), (5, keys.at[0, 13:16]), (6, keys.at[0, 4:8]), (7, keys.at[0, 9:13]),
-        (8, zrecv.at[1:NZ]), (9, keys.at[0, 0:4]), (10, keys.at[0, 13:16]),
-        (11, grecv.at[1:NXY]), (12, precv.at[1:32]), (13, hrecv.at[1:4]),
+        (0, keys.at[0, 1:NZ]), (2, queries.at[1:NXY]), (3, drecv.at[1:NXY]), (1, zrecv.at[1:NZ]),
+        (4, grecv.at[1:NXY]), (5, precv.at[1:32]), (6, hrecv.at[1:4]),
     ):
         took(ref, send_sem.at[phase])
+
+    def sent_keys(distance, carry):
+        took(keys.at[0, 1], key_send.at[distance])
+        return carry
+
+    lax.fori_loop(1, NZ - z, sent_keys, 0)
 
 
 def shards(
     cache_latent, group_latent, group_query, decode_query, group_start, w_key, w_value, w_out
 ):
-    anywhere = pl.BlockSpec(memory_space=pl.ANY)
+    hbm = pl.BlockSpec(memory_space=pltpu.HBM)
     vmem = pl.BlockSpec(memory_space=pltpu.VMEM)
     return pl.pallas_call(
         kernel,
@@ -343,10 +393,11 @@
             jax.ShapeDtypeStruct((2, 8, 512), BF),
             jax.ShapeDtypeStruct((2, 2, 8, 512), BF),
         ),
-        in_specs=[pl.BlockSpec(memory_space=pltpu.SMEM)] + [anywhere] * 7,
+        in_specs=[hbm] * 8,
         out_specs=(vmem, vmem),
         scratch_shapes=[
-            pltpu.VMEM((2, 256, 576), BF),
+            pltpu.SMEM((2,), jnp.int32),
+            pltpu.VMEM((2, 576, 256), BF),
             pltpu.VMEM((2, 8, 576), BF),
             pltpu.VMEM((2, 8, 768), BF),
             pltpu.VMEM((2, 2, 8, 768), BF),
@@ -365,16 +416,25 @@
             pltpu.VMEM((NXY, 16, 640), BF),
             pltpu.VMEM((4, 16, 512), BF),
             pltpu.VMEM((4, 16, 512), BF),
+            pltpu.SemaphoreType.DMA((8,)),
             pltpu.SemaphoreType.DMA((7,)),
-            pltpu.SemaphoreType.DMA((14,)),
-            pltpu.SemaphoreType.DMA((14,)),
+            pltpu.SemaphoreType.DMA((7,)),
+            pltpu.SemaphoreType.DMA((NZ,)),
+            pltpu.SemaphoreType.DMA((NZ,)),
+            pltpu.SemaphoreType.REGULAR((NZ,)),
         ],
         compiler_params=pltpu.CompilerParams(
             collective_id=0, has_side_effects=True, vmem_limit_bytes=32 << 20
         ),
         name="latent_attention",
     )(
-        group_start, cache_latent, group_latent, group_query, decode_query, w_key, w_value, w_out
+        *(
+            pltpu.with_memory_space_constraint(array, pltpu.HBM)
+            for array in (
+                group_start, cache_latent.transpose(0, 2, 1), group_latent, group_query,
+                decode_query, w_key, w_value, w_out,
+            )
+        )
     )
 
 

time: 50.7 us -> 41.7 us (0.82)
  local copies, waits for them, and re-layouts: 9.16 us -> 1.22 us
  Pallas kernels: 40.4 us -> 39.7 us
    unnamed x17 -> x2, local copies, waits for them, and re-layouts: 9.16 us -> 1.22 us
    pallas_call x1, Pallas kernels: 40.4 us -> 39.7 us  [shards(): pl.pallas_call(kernel, out_shape=(jax.ShapeDtypeStruct((2, 8, 512), BF),...]
where the time goes in v2:
time: 41.7 us; the launch traced here: 41.5 us
  Pallas kernels  39.7 us (95%)
  local copies, waits for them, and re-layouts  1.22 us (3%)
  between operations  0.64 us (2%)
    pallas_call x1, Pallas kernels, shards(): pl.pallas_call(kernel, out_shape=(jax.ShapeDtypeStruct((2, 8, 512), BF),...  39.7 us
    unnamed x2, local copies, waits for them, and re-layouts  1.22 us

profile of v2, /device:TPU:1, one launch (start us, length us, event | category | flops | bytes accessed | tf_op | source)
XLA Modules:
  0.0 41.5 jit_solution(7432254815901627824)
XLA Ops:
  0.6 39.7 %latent_attention.1 = (bf16[2,8,512]{2,1,0:T(8,128)(2,1)S(1)}, bf16[2,2,8,512]{3,2,1,0:T(8,128)(2,1)S(1)}) custom-call(s32[2]{0:T(128)} %start_hbm.1, bf16[2,576,256]{2,1,0:T(8,128)(2,1)} %bitcast.1, bf16[2,8,576]{2,1,0:T(8,128)(2,1)} %glat_hbm.1, bf16[2,8,768]{2,1,0:T(8,128)(2,1)} %gq_hbm.1, bf16[2,2,8,768]{3,2,1,0:T(8,128)(2,1)} %dq_hbm.1, ...), custom_call_target="tpu_custom_call" | custom-call | tf_op jit(solution)/shard_map/latent_attention/pallas_call | solution.py:390
  40.3 0.6 %copy.12 = bf16[2,8,512]{2,1,0:T(8,128)(2,1)} copy(bf16[2,8,512]{2,1,0:T(8,128)(2,1)S(1)} %get-tuple-element.4) | data formatting | bytes 32768
  40.9 0.6 %copy.13 = bf16[2,2,8,512]{3,2,1,0:T(8,128)(2,1)} copy(bf16[2,2,8,512]{3,2,1,0:T(8,128)(2,1)S(1)} %get-tuple-element.5) | data formatting | bytes 65536

commit v3 on v2

--- a/solution.py
+++ b/solution.py
@@ -12,7 +12,8 @@
 ROPE = 64
 NOPE = 128
 WIDE = NOPE + ROPE
-HALF = 384
+PADDED = 640
+SPLIT = 256
 LOCAL = 4
 NZ = 16
 NXY = 8
@@ -61,7 +62,7 @@
     start_hbm, cache_hbm, glat_hbm, gq_hbm, dq_hbm, wk_hbm, wv_hbm, wo_hbm,
     group_out, decode_out,
     start, cache, glat, gq, dq, wk, wv, wo,
-    keys, queries, big_q, dsend, drecv, zrecv, psend, precv, gsend, grecv, hsend, hrecv,
+    keys_a, keys_b, queries, big_q, dsend, drecv, zrecv, zstat, psend, precv, gsend, grecv, hsend, hrecv,
     local_sem, send_sem, recv_sem, key_send, key_recv, here,
 ):
     ctx = lax.axis_index("ctx")
@@ -102,18 +103,19 @@
         ("wo", wo_hbm, wo),
     )):
         loads[name] = pltpu.make_async_copy(src, dst, local_sem.at[at])
-        loads[name].start()
-    keys[...] = jnp.zeros_like(keys)
+        if name != "wo":
+            loads[name].start()
+    keys_a[...] = jnp.zeros_like(keys_a)
+    keys_b[...] = jnp.zeros_like(keys_b)
     barrier = pltpu.get_barrier_semaphore()
 
     def greet(device):
         pl.semaphore_signal(barrier, inc=1, device_id=device, device_id_type=MESH)
 
     def ranked(r):
-        return r % 2 * ((r + 1) // 2) + (1 - r % 2) * ((NZ - r // 2) % NZ)
-
-    upper = z // 9
-    rank = 2 * (z + upper * (NZ - 2 * z)) - 1 + upper + (NZ - z) // NZ
+        return r
+
+    rank = z
 
     def greet_z(r, carry):
         greet((ranked(r) * NXY + xy, head))
@@ -127,17 +129,24 @@
 
     loads["glat"].wait()
     own = glat[...].astype(F32).reshape(16, LAT + ROPE).astype(BF)
-    keys[0, 0] = own[:, :HALF]
-    keys[1, 0] = jnp.concatenate(
-        [own[:, HALF:], jnp.zeros((16, 2 * HALF - LAT - ROPE), BF)], axis=1
-    )
+    keys_a[0] = own[:, :SPLIT]
+    keys_b[0] = jnp.concatenate([own[:, SPLIT:], jnp.zeros((16, PADDED - LAT - ROPE), BF)], axis=1)
+
+    def on_core(action):
+        for at, keys in enumerate((keys_a, keys_b)):
+
+            @pl.when(core == at)
+            def _(keys=keys):
+                action(keys)
 
     def send_keys(there):
-        pltpu.make_async_remote_copy(
-            src_ref=keys.at[core, 0], dst_ref=keys.at[core, there - z],
-            send_sem=key_send.at[there - z], recv_sem=key_recv.at[there - z],
-            device_id=(there * NXY + xy, head), device_id_type=MESH,
-        ).start()
+        on_core(
+            lambda keys: pltpu.make_async_remote_copy(
+                src_ref=keys.at[0], dst_ref=keys.at[there - z],
+                send_sem=key_send.at[there - z], recv_sem=key_recv.at[there - z],
+                device_id=(there * NXY + xy, head), device_id_type=MESH,
+            ).start()
+        )
 
     def to_lower(r, carry):
         there = ranked(r)
@@ -154,35 +163,42 @@
 
         return carry
 
-    def to_higher(r, carry):
+    def send_z(there):
+        slot = (z - there + NZ) % NZ
+        remote(zrecv.at[0], zrecv.at[slot], 1, (there * NXY + xy, head))
+        remote(zstat.at[0], zstat.at[slot], 7, (there * NXY + xy, head))
+
+    def part_to_lower(r, carry):
+        send_z(ranked(r))
+        return carry
+
+    def to_higher(j, carry):
+        there = (z + (j + 1) // 2 * (2 * (j % 2) - 1) + NZ) % NZ
+
+        @pl.when(there > rank)
+        def _():
+            @pl.when(there > z + 3)
+            def _():
+                pl.semaphore_wait(here.at[there], 1)
+                send_keys(there)
+
+            send_z(there)
+
+        return carry
+
+    def keys_to_next(there, carry):
+        pl.semaphore_wait(here.at[there], 1)
+        send_keys(there)
+        return carry
+
+    def from_lower(r, carry):
         there = ranked(r)
-
-        @pl.when(there > z)
-        def _():
-            pl.semaphore_wait(here.at[there], 1)
-            send_keys(there)
 
         @pl.when(there < z)
         def _():
-            took(keys.at[0, 1], key_recv.at[z - there])
-
-        return carry
-
-    def from_lower(r, carry):
-        there = ranked(r)
-
-        @pl.when(there < z)
-        def _():
-            took(keys.at[0, 1], key_recv.at[z - there])
-
-        return carry
-
-    pl.semaphore_wait(barrier, 10 + rank)
-    lax.fori_loop(0, rank, to_lower, 0)
-    loads["gq"].wait()
-    queries[0] = gq[...].astype(F32).reshape(16, LOCAL * WIDE).astype(BF)
-    for rel in range(NXY - 1, 0, -1):
-        remote(queries.at[0], queries.at[back(rel)], 2, (xy_device(rel), head))
+            on_core(lambda keys: took(keys.at[1], key_recv.at[z - there]))
+
+        return carry
 
     loads["dq"].wait()
     rows = NXY * 16
@@ -242,8 +258,32 @@
     packed = jnp.concatenate([part, stats], axis=1).astype(BF).reshape(NXY, 16, 256)
     dsend[...] = packed
     drecv[0] = packed[0]
-    for rel in range(NXY - 1, 0, -1):
+    pl.semaphore_wait(barrier, 10 + rank)
+    for rel in (6, 2, 5, 7, 4, 1, 3):
         remote(dsend.at[rel], drecv.at[back(rel)], 3, (xy_device(rel), head))
+
+    lax.fori_loop(0, rank, to_lower, 0)
+    loads["gq"].wait()
+    queries[0] = gq[...].astype(F32).reshape(16, LOCAL * WIDE).astype(BF)
+    for rel in (6, 2, 5, 7, 4, 1, 3):
+        remote(queries.at[0], queries.at[back(rel)], 2, (xy_device(rel), head))
+
+    loads["wo"].start()
+
+    lax.fori_loop(z + 1, jnp.minimum(z + 4, NZ), keys_to_next, 0)
+
+    took(drecv.at[1:NXY], recv_sem.at[3])
+    packed = drecv[...].astype(F32)
+    peak, total, part = merge(packed[..., 128:], 0, packed[..., :128])
+    zrecv[0] = part.astype(BF)
+    lane, row = iota((16, 128), 1), iota((16, 128), 0)
+    zstat[0] = jnp.sum(
+        jnp.where(lane == row, peak, jnp.where(lane == row + 16, total, 0.0)),
+        axis=0, keepdims=True,
+    )
+
+    lax.fori_loop(0, rank, part_to_lower, 0)
+    lax.fori_loop(1, NZ, to_higher, 0)
 
     took(queries.at[1:NXY], recv_sem.at[2])
     all_q = queries[...].reshape(128, LOCAL * WIDE)
@@ -253,33 +293,23 @@
         big_q[h * 128 : (h + 1) * 128, LAT:] = jnp.concatenate(
             [
                 all_q[:, h * WIDE + NOPE : (h + 1) * WIDE],
-                jnp.zeros((128, 2 * HALF - LAT - ROPE), BF),
+                jnp.zeros((128, PADDED - LAT - ROPE), BF),
             ],
             axis=1,
         )
 
-    lax.fori_loop(rank + 1, NZ, to_higher, 0)
-
-    took(drecv.at[1:NXY], recv_sem.at[3])
-    packed = drecv[...].astype(F32)
-    peak, total, part = merge(packed[..., 128:], 0, packed[..., :128])
-    stats = by_lane((16, 128), dict(enumerate(split(peak, 3) + split(total, 2))))
-    zrecv[0] = jnp.concatenate([part, stats], axis=1).astype(BF)
-
-    def send_z(j, carry):
-        d = 8 + (j % 2 * 2 - 1) * ((j + 1) // 2)
-        remote(zrecv.at[0], zrecv.at[NZ - d], 1, (z_device(d), head))
-        return carry
-
-    lax.fori_loop(0, NZ - 1, send_z, 0)
-
     lax.fori_loop(0, rank, from_lower, 0)
-    remote(keys.at[core, 1:NZ], keys.at[core, 1:NZ], 0, (ctx, sibling))
-    took(keys.at[0, 1:NZ], recv_sem.at[0])
-
-    first = keys[0].reshape(256, HALF)
-    second = keys[1].reshape(256, HALF)
-    scores = dot_t(big_q[:, :HALF], first) + dot_t(big_q[:, HALF:], second)
+    on_core(lambda keys: remote(keys.at[1:NZ], keys.at[1:NZ], 0, (ctx, sibling)))
+    for at, keys in enumerate((keys_b, keys_a)):
+
+        @pl.when(core == at)
+        def _(keys=keys):
+            took(keys.at[1:NZ], recv_sem.at[0])
+
+
+    first = keys_a[...].reshape(256, SPLIT)
+    second = keys_b[...].reshape(256, PADDED - SPLIT)
+    scores = dot_t(big_q[:, :SPLIT], first) + dot_t(big_q[:, SPLIT:], second)
     row = iota((LOCAL * 128, 1), 0)
     col = iota((1, 256), 1)
     query_at = (z * NXY + absolute(row // 16 % NXY)) * 8 + row % 8
@@ -292,7 +322,7 @@
     total = jnp.sum(weights, axis=1, keepdims=True)
     weights = weights.astype(BF)
     mixture = jnp.concatenate(
-        [dot(weights, first), dot(weights, second[:, : LAT - HALF])], axis=1
+        [dot(weights, first), dot(weights, second[:, : LAT - SPLIT])], axis=1
     ).astype(BF)
     columns = {}
     for h in range(LOCAL):
@@ -305,13 +335,17 @@
     stats = by_lane((128, 128), columns).astype(BF).reshape(NXY, 16, 128)
     gsend[:, :, LAT:] = stats
     grecv[0, :, LAT:] = stats[0]
-    for rel in range(NXY - 1, 0, -1):
+    for rel in (6, 2, 5, 7, 4, 1, 3):
         remote(gsend.at[rel], grecv.at[back(rel)], 4, (xy_device(rel), head))
 
     took(zrecv.at[1:NZ], recv_sem.at[1])
-    packed = zrecv[...].astype(F32)
-    peak, total, part = merge(packed[..., 128:], 0, packed[..., :128])
-    attention = (part / total).astype(BF)
+    took(zstat.at[1:NZ], recv_sem.at[7])
+    lane, row = iota((NZ, 16, 128), 2), iota((NZ, 16, 128), 1)
+    peak = jnp.sum(jnp.where(lane == row, zstat[...], 0.0), axis=2, keepdims=True)
+    total = jnp.sum(jnp.where(lane == row + 16, zstat[...], 0.0), axis=2, keepdims=True)
+    factor = jnp.exp(peak - jnp.max(peak, axis=0, keepdims=True))
+    part = jnp.sum(factor * zrecv[...].astype(F32), axis=0)
+    attention = (part / jnp.sum(factor * total, axis=0)).astype(BF)
     row = iota((64, 16), 0)
     pick = row // 16 * 4 + row % 4 == iota((64, 16), 1)
     spread = dot(jnp.where(pick, 1.0, 0.0).astype(BF), attention).astype(BF)
@@ -327,15 +361,16 @@
         psend[j] = tile.astype(BF)
     precv[0] = psend[head]
 
-    def send_plane(j, carry):
-        k = 31 - j
-        rel, turn = k // 4, k % 4
+    for turn in (2, 1, 3, 0):
         there = (head + turn) % 4
-        slot = back(rel) * 4 + (4 - turn) % 4
-        remote(psend.at[there], precv.at[slot], 5, (xy_device(rel), there))
-        return carry
-
-    lax.fori_loop(0, 31, send_plane, 0)
+
+        def send_plane(j, carry, turn=turn, there=there):
+            rel = (j + 6) % NXY if turn else NXY - 1 - j
+            slot = back(rel) * 4 + (4 - turn) % 4
+            remote(psend.at[there], precv.at[slot], 5, (xy_device(rel), there))
+            return carry
+
+        lax.fori_loop(0, NXY if turn else NXY - 1, send_plane, 0)
 
     took(grecv.at[1:NXY], recv_sem.at[4])
     stats = grecv[:, :, LAT:].astype(F32)
@@ -370,13 +405,16 @@
     )
 
     for phase, ref in (
-        (0, keys.at[0, 1:NZ]), (2, queries.at[1:NXY]), (3, drecv.at[1:NXY]), (1, zrecv.at[1:NZ]),
+        (2, queries.at[1:NXY]), (3, drecv.at[1:NXY]), (1, zrecv.at[1:NZ]),
+        (7, zstat.at[1:NZ]),
         (4, grecv.at[1:NXY]), (5, precv.at[1:32]), (6, hrecv.at[1:4]),
     ):
         took(ref, send_sem.at[phase])
 
+    on_core(lambda keys: took(keys.at[1:NZ], send_sem.at[0]))
+
     def sent_keys(distance, carry):
-        took(keys.at[0, 1], key_send.at[distance])
+        on_core(lambda keys: took(keys.at[1], key_send.at[distance]))
         return carry
 
     lax.fori_loop(1, NZ - z, sent_keys, 0)
@@ -404,12 +442,14 @@
             pltpu.VMEM((512, 512), BF),
             pltpu.VMEM((512, 512), BF),
             pltpu.VMEM((512, 2048), BF),
-            pltpu.VMEM((2, NZ, 16, HALF), BF),
+            pltpu.VMEM((NZ, 16, SPLIT), BF),
+            pltpu.VMEM((NZ, 16, PADDED - SPLIT), BF),
             pltpu.VMEM((NXY, 16, 768), BF),
-            pltpu.VMEM((512, 2 * HALF), BF),
+            pltpu.VMEM((512, PADDED), BF),
             pltpu.VMEM((NXY, 16, 256), BF),
             pltpu.VMEM((NXY, 16, 256), BF),
-            pltpu.VMEM((NZ, 16, 256), BF),
+            pltpu.VMEM((NZ, 16, 128), BF),
+            pltpu.VMEM((NZ, 1, 128), F32),
             pltpu.VMEM((4, 16, 128), BF),
             pltpu.VMEM((32, 16, 128), BF),
             pltpu.VMEM((NXY, 16, 640), BF),
@@ -417,8 +457,8 @@
             pltpu.VMEM((4, 16, 512), BF),
             pltpu.VMEM((4, 16, 512), BF),
             pltpu.SemaphoreType.DMA((8,)),
-            pltpu.SemaphoreType.DMA((7,)),
-            pltpu.SemaphoreType.DMA((7,)),
+            pltpu.SemaphoreType.DMA((8,)),
+            pltpu.SemaphoreType.DMA((8,)),
             pltpu.SemaphoreType.DMA((NZ,)),
             pltpu.SemaphoreType.DMA((NZ,)),
             pltpu.SemaphoreType.REGULAR((NZ,)),

time: 41.7 us -> 38.4 us (0.921)
  the two profiles are of different devices: /device:TPU:1 before, /device:TPU:288 now
where the time goes in v3:
time: 38.4 us; the launch traced here: 38.2 us
  Pallas kernels  36.4 us (95%)
  local copies, waits for them, and re-layouts  1.22 us (3%)
  between operations  0.64 us (2%)
    pallas_call x1, Pallas kernels, shards(): pl.pallas_call(kernel, out_shape=(jax.ShapeDtypeStruct((2, 8, 512), BF),...  36.4 us
    unnamed x2, local copies, waits for them, and re-layouts  1.22 us

profile of v3, /device:TPU:288, one launch (start us, length us, event | category | flops | bytes accessed | tf_op | source)
XLA Modules:
  0.0 38.2 jit_solution(4716346894734215709)
XLA Ops:
  0.6 36.4 %latent_attention.1 = (bf16[2,8,512]{2,1,0:T(8,128)(2,1)S(1)}, bf16[2,2,8,512]{3,2,1,0:T(8,128)(2,1)S(1)}) custom-call(s32[2]{0:T(128)} %start_hbm.1, bf16[2,576,256]{2,1,0:T(8,128)(2,1)} %bitcast.1, bf16[2,8,576]{2,1,0:T(8,128)(2,1)} %glat_hbm.1, bf16[2,8,768]{2,1,0:T(8,128)(2,1)} %gq_hbm.1, bf16[2,2,8,768]{3,2,1,0:T(8,128)(2,1)} %dq_hbm.1, ...), custom_call_target="tpu_custom_call" | custom-call | tf_op jit(solution)/shard_map/latent_attention/pallas_call | solution.py:428
  37.0 0.6 %copy.12 = bf16[2,8,512]{2,1,0:T(8,128)(2,1)} copy(bf16[2,8,512]{2,1,0:T(8,128)(2,1)S(1)} %get-tuple-element.4) | data formatting | bytes 32768
  37.6 0.6 %copy.13 = bf16[2,2,8,512]{3,2,1,0:T(8,128)(2,1)} copy(bf16[2,2,8,512]{3,2,1,0:T(8,128)(2,1)S(1)} %get-tuple-element.5) | data formatting | bytes 65536

commit v4 on v3

--- a/solution.py
+++ b/solution.py
@@ -62,7 +62,8 @@
     start_hbm, cache_hbm, glat_hbm, gq_hbm, dq_hbm, wk_hbm, wv_hbm, wo_hbm,
     group_out, decode_out,
     start, cache, glat, gq, dq, wk, wv, wo,
-    keys_a, keys_b, queries, big_q, dsend, drecv, zrecv, zstat, psend, precv, gsend, grecv, hsend, hrecv,
+    keys_a, keys_b, queries, big_q, dsend, drecv, zrecv, zstat, final, psend, precv,
+    gsend, grecv, hsend, hrecv,
     local_sem, send_sem, recv_sem, key_send, key_recv, here,
 ):
     ctx = lax.axis_index("ctx")
@@ -169,19 +170,27 @@
         remote(zstat.at[0], zstat.at[slot], 7, (there * NXY + xy, head))
 
     def part_to_lower(r, carry):
-        send_z(ranked(r))
-        return carry
-
-    def to_higher(j, carry):
-        there = (z + (j + 1) // 2 * (2 * (j % 2) - 1) + NZ) % NZ
-
-        @pl.when(there > rank)
+        send_z(r)
+        return carry
+
+    def ahead(j):
+        return (z + (j + 1) // 2 * (2 * (j % 2) - 1) + NZ) % NZ
+
+    def keys_to_higher(j, carry):
+        there = ahead(j)
+
+        @pl.when(there > z + 3)
         def _():
-            @pl.when(there > z + 3)
-            def _():
-                pl.semaphore_wait(here.at[there], 1)
-                send_keys(there)
-
+            pl.semaphore_wait(here.at[there], 1)
+            send_keys(there)
+
+        return carry
+
+    def part_to_higher(j, carry):
+        there = ahead(j)
+
+        @pl.when((there > z) & (there < 8))
+        def _():
             send_z(there)
 
         return carry
@@ -282,8 +291,9 @@
         axis=0, keepdims=True,
     )
 
-    lax.fori_loop(0, rank, part_to_lower, 0)
-    lax.fori_loop(1, NZ, to_higher, 0)
+    lax.fori_loop(0, jnp.minimum(z, 8), part_to_lower, 0)
+    lax.fori_loop(1, NZ, keys_to_higher, 0)
+    lax.fori_loop(1, NZ, part_to_higher, 0)
 
     took(queries.at[1:NXY], recv_sem.at[2])
     all_q = queries[...].reshape(128, LOCAL * WIDE)
@@ -338,14 +348,23 @@
     for rel in (6, 2, 5, 7, 4, 1, 3):
         remote(gsend.at[rel], grecv.at[back(rel)], 4, (xy_device(rel), head))
 
-    took(zrecv.at[1:NZ], recv_sem.at[1])
-    took(zstat.at[1:NZ], recv_sem.at[7])
-    lane, row = iota((NZ, 16, 128), 2), iota((NZ, 16, 128), 1)
-    peak = jnp.sum(jnp.where(lane == row, zstat[...], 0.0), axis=2, keepdims=True)
-    total = jnp.sum(jnp.where(lane == row + 16, zstat[...], 0.0), axis=2, keepdims=True)
-    factor = jnp.exp(peak - jnp.max(peak, axis=0, keepdims=True))
-    part = jnp.sum(factor * zrecv[...].astype(F32), axis=0)
-    attention = (part / jnp.sum(factor * total, axis=0)).astype(BF)
+    @pl.when(z < 8)
+    def _():
+        took(zrecv.at[1:NZ], recv_sem.at[1])
+        took(zstat.at[1:NZ], recv_sem.at[7])
+        lane, row = iota((NZ, 16, 128), 2), iota((NZ, 16, 128), 1)
+        peak = jnp.sum(jnp.where(lane == row, zstat[...], 0.0), axis=2, keepdims=True)
+        total = jnp.sum(jnp.where(lane == row + 16, zstat[...], 0.0), axis=2, keepdims=True)
+        factor = jnp.exp(peak - jnp.max(peak, axis=0, keepdims=True))
+        part = jnp.sum(factor * zrecv[...].astype(F32), axis=0)
+        final[...] = (part / jnp.sum(factor * total, axis=0)).astype(BF)
+        remote(final, final, 8, ((z + 8) * NXY + xy, head))
+
+    @pl.when(z >= 8)
+    def _():
+        took(final, recv_sem.at[8])
+
+    attention = final[...]
     row = iota((64, 16), 0)
     pick = row // 16 * 4 + row % 4 == iota((64, 16), 1)
     spread = dot(jnp.where(pick, 1.0, 0.0).astype(BF), attention).astype(BF)
@@ -405,13 +424,23 @@
     )
 
     for phase, ref in (
-        (2, queries.at[1:NXY]), (3, drecv.at[1:NXY]), (1, zrecv.at[1:NZ]),
-        (7, zstat.at[1:NZ]),
+        (2, queries.at[1:NXY]), (3, drecv.at[1:NXY]),
         (4, grecv.at[1:NXY]), (5, precv.at[1:32]), (6, hrecv.at[1:4]),
     ):
         took(ref, send_sem.at[phase])
 
     on_core(lambda keys: took(keys.at[1:NZ], send_sem.at[0]))
+
+    @pl.when(z < 8)
+    def _():
+        took(zrecv.at[1:8], send_sem.at[1])
+        took(zstat.at[1:8], send_sem.at[7])
+        took(final, send_sem.at[8])
+
+    @pl.when(z >= 8)
+    def _():
+        took(zrecv.at[1:9], send_sem.at[1])
+        took(zstat.at[1:9], send_sem.at[7])
 
     def sent_keys(distance, carry):
         on_core(lambda keys: took(keys.at[1], key_send.at[distance]))
@@ -450,6 +479,7 @@
             pltpu.VMEM((NXY, 16, 256), BF),
             pltpu.VMEM((NZ, 16, 128), BF),
             pltpu.VMEM((NZ, 1, 128), F32),
+            pltpu.VMEM((16, 128), BF),
             pltpu.VMEM((4, 16, 128), BF),
             pltpu.VMEM((32, 16, 128), BF),
             pltpu.VMEM((NXY, 16, 640), BF),
@@ -457,8 +487,8 @@
             pltpu.VMEM((4, 16, 512), BF),
             pltpu.VMEM((4, 16, 512), BF),
             pltpu.SemaphoreType.DMA((8,)),
-            pltpu.SemaphoreType.DMA((8,)),
-            pltpu.SemaphoreType.DMA((8,)),
+            pltpu.SemaphoreType.DMA((9,)),
+            pltpu.SemaphoreType.DMA((9,)),
             pltpu.SemaphoreType.DMA((NZ,)),
             pltpu.SemaphoreType.DMA((NZ,)),
             pltpu.SemaphoreType.REGULAR((NZ,)),

time: 38.4 us -> 37.2 us (0.969)
  the two profiles are of different devices: /device:TPU:288 before, /device:TPU:385 now
where the time goes in v4:
time: 37.2 us; the launch traced here: 37 us
  Pallas kernels  35.2 us (95%)
  local copies, waits for them, and re-layouts  1.22 us (3%)
  between operations  0.64 us (2%)
    pallas_call x1, Pallas kernels, shards(): pl.pallas_call(kernel, out_shape=(jax.ShapeDtypeStruct((2, 8, 512), BF),...  35.2 us
    unnamed x2, local copies, waits for them, and re-layouts  1.22 us

profile of v4, /device:TPU:385, one launch (start us, length us, event | category | flops | bytes accessed | tf_op | source)
XLA Modules:
  0.0 37.0 jit_solution(14796085059214637817)
XLA Ops:
  0.6 35.2 %latent_attention.1 = (bf16[2,8,512]{2,1,0:T(8,128)(2,1)S(1)}, bf16[2,2,8,512]{3,2,1,0:T(8,128)(2,1)S(1)}) custom-call(s32[2]{0:T(128)} %start_hbm.1, bf16[2,576,256]{2,1,0:T(8,128)(2,1)} %bitcast.1, bf16[2,8,576]{2,1,0:T(8,128)(2,1)} %glat_hbm.1, bf16[2,8,768]{2,1,0:T(8,128)(2,1)} %gq_hbm.1, bf16[2,2,8,768]{3,2,1,0:T(8,128)(2,1)} %dq_hbm.1, ...), custom_call_target="tpu_custom_call" | custom-call | tf_op jit(solution)/shard_map/latent_attention/pallas_call | solution.py:457
  35.8 0.6 %copy.12 = bf16[2,8,512]{2,1,0:T(8,128)(2,1)} copy(bf16[2,8,512]{2,1,0:T(8,128)(2,1)S(1)} %get-tuple-element.4) | data formatting | bytes 32768
  36.4 0.6 %copy.13 = bf16[2,2,8,512]{3,2,1,0:T(8,128)(2,1)} copy(bf16[2,2,8,512]{3,2,1,0:T(8,128)(2,1)S(1)} %get-tuple-element.5) | data formatting | bytes 65536

commit v5 on v4

--- a/solution.py
+++ b/solution.py
@@ -114,9 +114,12 @@
         pl.semaphore_signal(barrier, inc=1, device_id=device, device_id_type=MESH)
 
     def ranked(r):
-        return r
-
-    rank = z
+        return jnp.where(r < 6, r, jnp.where(r < 10, r + 6, r - 4))
+
+    def rank_of(there):
+        return jnp.where(there < 6, there, jnp.where(there < 12, there + 4, there - 6))
+
+    rank = rank_of(z)
 
     def greet_z(r, carry):
         greet((ranked(r) * NXY + xy, head))
@@ -152,7 +155,7 @@
     def to_lower(r, carry):
         there = ranked(r)
 
-        @pl.when(there > z)
+        @pl.when((there > z) & (z < 8))
         def _():
             send_keys(there)
 
@@ -179,13 +182,17 @@
     def keys_to_higher(j, carry):
         there = ahead(j)
 
-        @pl.when(there > z + 3)
+        @pl.when((there > z + 3) & (rank_of(there) > rank))
         def _():
             pl.semaphore_wait(here.at[there], 1)
             send_keys(there)
 
         return carry
 
+    def keys_direct(there, carry):
+        send_keys(there)
+        return carry
+
     def part_to_higher(j, carry):
         there = ahead(j)
 
@@ -196,14 +203,15 @@
         return carry
 
     def keys_to_next(there, carry):
-        pl.semaphore_wait(here.at[there], 1)
-        send_keys(there)
-        return carry
-
-    def from_lower(r, carry):
-        there = ranked(r)
-
-        @pl.when(there < z)
+        @pl.when(rank_of(there) > rank)
+        def _():
+            pl.semaphore_wait(here.at[there], 1)
+            send_keys(there)
+
+        return carry
+
+    def from_lower(there, carry):
+        @pl.when((z < 12) | (there // 2 != 3))
         def _():
             on_core(lambda keys: took(keys.at[1], key_recv.at[z - there]))
 
@@ -291,9 +299,20 @@
         axis=0, keepdims=True,
     )
 
-    lax.fori_loop(0, jnp.minimum(z, 8), part_to_lower, 0)
+    lax.fori_loop(0, jnp.where(z < 12, jnp.minimum(z, 8), 6), part_to_lower, 0)
+    @pl.when(z // 4 == 2)
+    def _():
+        lax.fori_loop(12, NZ, keys_direct, 0)
+
     lax.fori_loop(1, NZ, keys_to_higher, 0)
     lax.fori_loop(1, NZ, part_to_higher, 0)
+
+    @pl.when(z >= 12)
+    def _():
+        for there in (7, 6):
+            on_core(lambda keys, there=there: took(keys.at[1], key_recv.at[z - there]))
+            send_z(there)
+
 
     took(queries.at[1:NXY], recv_sem.at[2])
     all_q = queries[...].reshape(128, LOCAL * WIDE)
@@ -308,7 +327,7 @@
             axis=1,
         )
 
-    lax.fori_loop(0, rank, from_lower, 0)
+    lax.fori_loop(0, z, from_lower, 0)
     on_core(lambda keys: remote(keys.at[1:NZ], keys.at[1:NZ], 0, (ctx, sibling)))
     for at, keys in enumerate((keys_b, keys_a)):
 

time: 37.2 us -> 38.8 us (1.043)
  the two profiles are of different devices: /device:TPU:385 before, /device:TPU:481 now
where the time goes in v5:
time: 38.8 us; the launch traced here: 38.7 us
  Pallas kernels  36.8 us (95%)
  local copies, waits for them, and re-layouts  1.22 us (3%)
  between operations  0.64 us (2%)
    pallas_call x1, Pallas kernels, shards(): pl.pallas_call(kernel, out_shape=(jax.ShapeDtypeStruct((2, 8, 512), BF),...  36.8 us
    unnamed x2, local copies, waits for them, and re-layouts  1.22 us

profile of v5, /device:TPU:481, one launch (start us, length us, event | category | flops | bytes accessed | tf_op | source)
XLA Modules:
  0.0 38.7 jit_solution(3977059915899349735)
XLA Ops:
  0.6 36.8 %latent_attention.1 = (bf16[2,8,512]{2,1,0:T(8,128)(2,1)S(1)}, bf16[2,2,8,512]{3,2,1,0:T(8,128)(2,1)S(1)}) custom-call(s32[2]{0:T(128)} %start_hbm.1, bf16[2,576,256]{2,1,0:T(8,128)(2,1)} %bitcast.1, bf16[2,8,576]{2,1,0:T(8,128)(2,1)} %glat_hbm.1, bf16[2,8,768]{2,1,0:T(8,128)(2,1)} %gq_hbm.1, bf16[2,2,8,768]{3,2,1,0:T(8,128)(2,1)} %dq_hbm.1, ...), custom_call_target="tpu_custom_call" | custom-call | tf_op jit(solution)/shard_map/latent_attention/pallas_call | solution.py:476
  37.5 0.6 %copy.12 = bf16[2,8,512]{2,1,0:T(8,128)(2,1)} copy(bf16[2,8,512]{2,1,0:T(8,128)(2,1)S(1)} %get-tuple-element.4) | data formatting | bytes 32768
  38.1 0.6 %copy.13 = bf16[2,2,8,512]{3,2,1,0:T(8,128)(2,1)} copy(bf16[2,2,8,512]{3,2,1,0:T(8,128)(2,1)S(1)} %get-tuple-element.5) | data formatting | bytes 65536
